TPU v7x, 32 devices: a whole 2x2x4 slice. The times are simulated.
32 devices in a mesh: gx: 4 (over y, core), gy: 4 (over z), gz: 2 (over x).
Axes of the slice: x: 2, y: 2, z: 4, core: 2. Of those that a mesh axis runs over, the one named last changes fastest.
Arguments:
- fine_disp: float32 [3, 8, 128, 2048], P(None, None, ('gy', 'gz'), 'gx'), may hold values from -6 to 6
- fine_prev: float32 [3, 8, 128, 2048], P(None, None, ('gy', 'gz'), 'gx'), may hold values from -6 to 6
- fine_media: float32 [4, 8, 128, 2048], P(None, None, ('gy', 'gz'), 'gx'), may hold values from 0.5 to 2
- coarse_disp: float32 [3, 8, 64, 1024], P(None, None, 'gy', ('gx', 'gz')), may hold values from -6 to 6
- coarse_prev: float32 [3, 8, 64, 1024], P(None, None, 'gy', ('gx', 'gz')), may hold values from -6 to 6
- coarse_media: float32 [3, 8, 64, 1024], P(None, None, 'gy', ('gx', 'gz')), may hold values from 0.5 to 2
- source_cell: int32 [4, 8, 8192], P('gx', ('gy', 'gz')), may hold values from 0 to 8191, as said below
- target_cell: int32 [4, 8, 8192], P('gx', ('gy', 'gz')), may hold values from 0 to 2047, as said below
- target_owner: int32 [4, 8, 8192], P('gx', ('gy', 'gz')), may hold values from 0 to 7, as said below
- target_weight: float32 [4, 8, 8192], P('gx', ('gy', 'gz')), may hold values from 0.1 to 0.4
- used_count: int32 [4, 8], P('gx', ('gy', 'gz')), may hold values from 4096 to 8192, as said below
Outputs:
- fine_next: float32 [3, 8, 128, 2048], P(None, None, ('gy', 'gz'), 'gx')
- coarse_next: float32 [3, 8, 64, 1024], P(None, None, 'gy', ('gx', 'gz'))
- ghost_plane: float32 [3, 64, 1024], P(None, 'gy', ('gx', 'gz'))
Inputs may be any that keep to these rules, and one draw needn't show every extreme that they name: `source_cell`: each block lists every cell of its bottom plane once, as y * 512 + x in the block, in an order drawn from the seed. `target_cell`: row * 128 + column in the owner's block of the ghost plane. `target_owner`: the owner has the same gy index as the device that holds the entry. `used_count`: entries at and past the count are padding.
All inputs are finite; a program needn't handle non-finite values.
Results may differ from a plain program's by a relative error of at most 0.000075.
Values sent between devices are 32-bit elements; how exact they have to be, the bound alone decides.
A program may use at most 64 MiB of HBM per device.

v0:
```python
import functools

import jax
import jax.numpy as jnp
from jax import lax
from jax.experimental import pallas as pl
from jax.experimental.pallas import tpu as pltpu
from jax.sharding import PartitionSpec as P

step_scale = 0.02
MESH = pl.DeviceIdType.MESH
CHUNK_ROWS = 8
EARLY_TURNS = 1


def rows_of(ref, start, count):
    return jnp.concatenate([ref[pl.ds(start + q, 1), :] for q in range(count)], axis=1)


def second(values):
    low2, low1, mid, high1, high2 = values
    return (16.0 * (low1 + high1) - (low2 + high2) - 30.0 * mid) * (1.0 / 12.0)


def pack_columns(ref, out_ref, first, lane0, depth, comps):
    rows = out_ref.shape[0]
    lane = lax.broadcasted_iota(jnp.int32, (rows, 128), 1) // 2
    total = jnp.zeros((rows, 128), jnp.float32)
    for c in range(comps):
        for z in range(depth):
            k = c * depth + z
            tile = ref[c, 2 + z, 8 : 8 + rows, first : first + 128]
            total = jnp.where(lane == k, pltpu.roll(tile, (2 * k - lane0) % 128, 1), total)
    out_ref[...] = total


def stencil_xy(ref, from_low, from_high, c, z, k):
    rows = from_low.shape[0]
    cols = ref.shape[3]
    wide = cols + 256
    mid = ref[c, 2 + z, 8 : 8 + rows, :]
    left = pltpu.roll(from_low[...], 126 - 2 * k, 1)
    right = pltpu.roll(from_high[...], (128 - 2 * k) % 128, 1)
    ext = jnp.concatenate([left, mid, right], axis=1)
    moved = [pltpu.roll(ext, s % wide, 1)[:, 128 : 128 + cols] for s in (2, 1, -1, -2)]
    along_x = second((moved[0], moved[1], mid, moved[2], moved[3]))
    shifted = [ref[c, 2 + z, 6 + s : 6 + s + rows, :] for s in (0, 1, 3, 4)]
    along_y = second((shifted[0], shifted[1], mid, shifted[2], shifted[3]))
    along_z = second(
        (
            ref[c, z, 8 : 8 + rows, :],
            ref[c, z + 1, 8 : 8 + rows, :],
            mid,
            ref[c, z + 3, 8 : 8 + rows, :],
            ref[c, z + 4, 8 : 8 + rows, :],
        )
    )
    return mid, along_x, along_y, along_z


def kernel(
    sizes,
    count_hbm,
    fine_hbm,
    fprev_hbm,
    fmedia_hbm,
    coarse_hbm,
    cprev_hbm,
    cmedia_hbm,
    source_hbm,
    target_hbm,
    owner_hbm,
    weight_hbm,
    fnext,
    cnext,
    ghost,
    count_ref,
    fp,
    fprev,
    fmedia,
    cp,
    cprev,
    cmedia,
    source,
    target,
    owner,
    weight,
    fy_out,
    fy_in,
    fx_out,
    fx_in,
    cy_out,
    cy_in,
    cx_out,
    cx_in,
    src_lo,
    src_hi,
    tgt_lo,
    tgt_hi,
    total,
    partial,
    peer_part,
    load_sem,
    send_sem,
    recv_sem,
):
    n_gx, n_gy, n_gz = sizes
    comps, depth, rows, cols = fprev.shape
    crows, ccols = cprev.shape[2:]
    gx = lax.axis_index("gx")
    gy = lax.axis_index("gy")
    gz = lax.axis_index("gz")

    loads = [
        (fine_hbm.at[:, depth - 1 :], fp.at[:, 1 + depth : 2 + depth, 8 : 8 + rows, :]),
        (source_hbm, source),
        (target_hbm, target),
        (owner_hbm, owner),
        (weight_hbm, weight),
        (count_hbm, count_ref),
        (fine_hbm.at[:, : depth - 1], fp.at[:, 2 : 1 + depth, 8 : 8 + rows, :]),
        (coarse_hbm, cp.at[:, 2 : 2 + depth, 8 : 8 + crows, :]),
        (fmedia_hbm, fmedia),
        (fprev_hbm, fprev),
        (cmedia_hbm, cmedia),
        (cprev_hbm, cprev),
    ]
    load = [pltpu.make_async_copy(a, b, load_sem.at[i]) for i, (a, b) in enumerate(loads)]
    for copy in load:
        copy.start()

    fine_y = gy * n_gz + gz
    coarse_x = gx * n_gz + gz
    has = [
        fine_y > 0,
        fine_y < n_gy * n_gz - 1,
        gx > 0,
        gx < n_gx - 1,
        gy > 0,
        gy < n_gy - 1,
        coarse_x > 0,
        coarse_x < n_gx * n_gz - 1,
    ]
    y_low, y_high = fine_y - 1, fine_y + 1
    x_low, x_high = coarse_x - 1, coarse_x + 1
    where_to = [
        (gx, lax.div(y_low, n_gz), lax.rem(y_low, n_gz)),
        (gx, lax.div(y_high, n_gz), lax.rem(y_high, n_gz)),
        (gx - 1, gy, gz),
        (gx + 1, gy, gz),
        (gx, gy - 1, gz),
        (gx, gy + 1, gz),
        (lax.div(x_low, n_gz), gy, lax.rem(x_low, n_gz)),
        (lax.div(x_high, n_gz), gy, lax.rem(x_high, n_gz)),
    ]
    buffers = [fy_out, fy_out, fx_out, fx_out, cy_out, cy_out, cx_out, cx_out]
    landing = [fy_in, fy_in, fx_in, fx_in, cy_in, cy_in, cx_in, cx_in]
    peer = (gx, gy, n_gz - 1 - gz)

    barrier = pltpu.get_barrier_semaphore()
    expected = 1
    pl.semaphore_signal(barrier, inc=1, device_id=peer, device_id_type=MESH)
    for n in range(8):
        expected = expected + has[n].astype(jnp.int32)

        @pl.when(has[n])
        def _():
            pl.semaphore_signal(barrier, inc=1, device_id=where_to[n], device_id_type=MESH)

        @pl.when(jnp.logical_not(has[n]))
        def _():
            landing[n][n % 2] = jnp.zeros(landing[n].shape[1:], jnp.float32)

    zero_fine = jnp.zeros((comps, 2, rows, cols), jnp.float32)
    fp[:, 0:2, 8 : 8 + rows, :] = zero_fine
    fp[:, 2 + depth : 4 + depth, 8 : 8 + rows, :] = zero_fine
    zero_coarse = jnp.zeros((comps, 2, crows, ccols), jnp.float32)
    cp[:, 0:2, 8 : 8 + crows, :] = zero_coarse
    cp[:, 2 + depth : 4 + depth, 8 : 8 + crows, :] = zero_coarse

    def halo(n):
        return pltpu.make_async_remote_copy(
            src_ref=buffers[n].at[n % 2],
            dst_ref=landing[n].at[1 - n % 2],
            send_sem=send_sem.at[n],
            recv_sem=recv_sem.at[n],
            device_id=where_to[n],
            device_id_type=MESH,
        )

    load[0].wait()
    half = 256
    halves = cols // half
    pieces = []
    for c in range(comps):
        for h in range(halves):
            pieces.append(fp[c, 1 + depth, 8 : 8 + rows, h * half : (h + 1) * half])
    plane = jnp.concatenate(pieces, axis=0)
    plane_high = plane.astype(jnp.bfloat16)
    plane_low = (plane - plane_high.astype(jnp.float32)).astype(jnp.bfloat16)
    plane = jnp.concatenate([plane_high, plane_low], axis=0)
    group = halves * rows

    for i in range(1, 6):
        load[i].wait()
    cell = source[...]
    src_lo[...] = (cell % half).astype(jnp.float32)
    src_hi[...] = ((cell % cols) // half * rows + cell // cols).astype(jnp.float32)
    cell = target[...]
    tgt_lo[...] = (cell % ccols).astype(jnp.float32)
    tgt_hi[...] = (owner[...] % n_gz * crows + cell // ccols).astype(jnp.float32)
    entry_rows = source.shape[0]
    place = lax.broadcasted_iota(jnp.int32, (entry_rows, 128), 0) * 128
    place = place + lax.broadcasted_iota(jnp.int32, (entry_rows, 128), 1)
    weight[...] = jnp.where(place < count_ref[0, 0], weight[...], 0.0)

    wide = CHUNK_ROWS * 128
    base = lax.broadcasted_iota(jnp.int32, (16, wide), 0).astype(jnp.float32).astype(jnp.bfloat16)
    group_base = lax.broadcasted_iota(jnp.int32, (group, wide), 0).astype(jnp.float32)
    one = jnp.ones((16, wide), jnp.bfloat16)
    zero = jnp.zeros((16, wide), jnp.bfloat16)
    total[...] = jnp.zeros_like(total)

    def spread(row):
        return jnp.broadcast_to(row, (16, wide)).astype(jnp.bfloat16)

    def onehot(ref, start, count):
        index = spread(rows_of(ref, start, CHUNK_ROWS))
        return jnp.concatenate(
            [jnp.where(index == base + float(16 * t), one, zero) for t in range(count // 16)],
            axis=0,
        )

    def add_entries(turn):
        start = turn * CHUNK_ROWS
        picked = jnp.dot(plane, onehot(src_lo, start, half), preferred_element_type=jnp.float32)
        picked = picked[: comps * group] + picked[comps * group :]
        row_mask = jnp.broadcast_to(rows_of(src_hi, start, CHUNK_ROWS), (group, wide)) == group_base
        scale = rows_of(weight, start, CHUNK_ROWS)
        target_row = spread(rows_of(tgt_hi, start, CHUNK_ROWS))
        masks = [target_row == base + float(16 * t) for t in range(n_gz * crows // 16)]
        high_part, low_part = [], []
        for c in range(comps):
            value = jnp.where(row_mask, picked[c * group : (c + 1) * group], 0.0)
            value = jnp.sum(value, axis=0, keepdims=True) * scale
            value = jnp.broadcast_to(value, (16, wide))
            high = value.astype(jnp.bfloat16)
            low = (value - high.astype(jnp.float32)).astype(jnp.bfloat16)
            high_part += [jnp.where(mask, high, zero) for mask in masks]
            low_part += [jnp.where(mask, low, zero) for mask in masks]
        total[...] += lax.dot_general(
            jnp.concatenate(high_part + low_part, axis=0),
            onehot(tgt_lo, start, ccols),
            (((1,), (1,)), ((), ())),
            preferred_element_type=jnp.float32,
        )

    turns = entry_rows // CHUNK_ROWS
    pl.loop(0, EARLY_TURNS)(add_entries)

    load[6].wait()
    for side, first in ((0, 8), (1, 8 + rows - 2)):
        fy_out[side] = fp[:, 2 : 2 + depth, first : first + 2, :]
    pack_columns(fp, fx_out.at[0], 0, 0, depth, comps)
    pack_columns(fp, fx_out.at[1], cols - 128, 126, depth, comps)
    load[7].wait()
    for side, first in ((0, 8), (1, 8 + crows - 2)):
        cy_out[side] = cp[:, 2 : 2 + depth, first : first + 2, :]
    pack_columns(cp, cx_out.at[0], 0, 0, depth, comps)
    pack_columns(cp, cx_out.at[1], ccols - 128, 126, depth, comps)
    pl.semaphore_wait(barrier, expected)
    for n in range(8):

        @pl.when(has[n])
        def _():
            halo(n).start()

    pl.loop(EARLY_TURNS, turns)(add_entries)

    span = n_gz * crows
    for c in range(comps):
        partial[c] = (
            total[c * span : (c + 1) * span, :] + total[(comps + c) * span : (comps + c + 1) * span, :]
        )
    swap = pltpu.make_async_remote_copy(
        src_ref=partial.at[:, pl.ds(pl.multiple_of((n_gz - 1 - gz) * crows, 8), crows), :],
        dst_ref=peer_part,
        send_sem=send_sem.at[8],
        recv_sem=recv_sem.at[8],
        device_id=peer,
        device_id_type=MESH,
    )
    swap.start()

    def arrive(n):
        @pl.when(has[n ^ 1])
        def _():
            halo(n).wait_recv()

    for n in range(4):
        arrive(n)
    fp[:, 2 : 2 + depth, 6:8, :] = fy_in[0]
    fp[:, 2 : 2 + depth, 8 + rows : 10 + rows, :] = fy_in[1]
    load[8].wait()
    load[9].wait()
    for z in range(depth):
        shear, first, density, metric = (fmedia[i, z] for i in range(4))
        scale = step_scale / density
        both = first + shear
        for c in range(comps):
            k = c * depth + z
            mid, along_x, along_y, along_z = stencil_xy(fp, fx_in.at[0], fx_in.at[1], c, z, k)
            along_z = metric * along_z
            along = (along_x, along_y, along_z)[c]
            accel = shear * (along_x + along_y + along_z) + both * along
            fnext[c, z] = 2.0 * mid - fprev[c, z] + scale * accel

    for n in range(4, 8):
        arrive(n)
    cp[:, 2 : 2 + depth, 6:8, :] = cy_in[0]
    cp[:, 2 : 2 + depth, 8 + crows : 10 + crows, :] = cy_in[1]
    load[10].wait()
    load[11].wait()
    for z in range(depth):
        shear, first, density = (cmedia[i, z] for i in range(3))
        scale = (step_scale / 4.0) / density
        both = first + shear
        for c in range(comps):
            k = c * depth + z
            mid, along_x, along_y, along_z = stencil_xy(cp, cx_in.at[0], cx_in.at[1], c, z, k)
            along = (along_x, along_y, along_z)[c]
            accel = shear * (along_x + along_y + along_z) + both * along
            cnext[c, z] = 2.0 * mid - cprev[c, z] + scale * accel

    swap.wait_recv()
    own = pl.ds(pl.multiple_of(gz * crows, 8), crows)
    for c in range(comps):
        column = partial[c, own, :] + peer_part[c]
        ghost[c] = column
        for z, share in ((0, 16.0 / 12.0), (1, -1.0 / 12.0)):
            shear, first, density = (cmedia[i, z] for i in range(3))
            factor = shear + (first + shear) if c == 2 else shear
            cnext[c, z] += (share * step_scale / 4.0) / density * factor * column

    for n in range(8):

        @pl.when(has[n])
        def _():
            halo(n).wait_send()

    swap.wait_send()


def store(fnext, cnext, ghost, fnext_hbm, cnext_hbm, ghost_hbm, sem):
    pairs = ((fnext, fnext_hbm), (cnext, cnext_hbm), (ghost, ghost_hbm))
    copies = [pltpu.make_async_copy(a, b, sem.at[i]) for i, (a, b) in enumerate(pairs)]
    for copy in copies:
        copy.start()
    for copy in copies:
        copy.wait()


def shards(
    sizes,
    fine_disp,
    fine_prev,
    fine_media,
    coarse_disp,
    coarse_prev,
    coarse_media,
    source_cell,
    target_cell,
    target_owner,
    target_weight,
    used_count,
):
    f32 = jnp.float32
    comps, depth, rows, cols = fine_disp.shape
    crows, ccols = coarse_disp.shape[2:]
    entries = source_cell.shape[-1]
    lists = [
        a.reshape(entries // 128, 128)
        for a in (source_cell, target_cell, target_owner, target_weight)
    ]
    entry = (entries // 128, 128)
    vm = pltpu.VMEM
    group = cols // 256 * rows
    n_gz = sizes[2]
    in_hbm = pl.BlockSpec(memory_space=pltpu.HBM)
    out_shape = (
        jax.ShapeDtypeStruct(fine_disp.shape, f32),
        jax.ShapeDtypeStruct(coarse_disp.shape, f32),
        jax.ShapeDtypeStruct((comps, crows, ccols), f32),
    )
    results = pl.pallas_call(
        functools.partial(kernel, sizes),
        out_shape=tuple(vm(o.shape, o.dtype) for o in out_shape),
        in_specs=[in_hbm] * 11,
        out_specs=(pl.BlockSpec(memory_space=pltpu.VMEM),) * 3,
        scratch_shapes=[
            pltpu.SMEM((1, 1), jnp.int32),
            vm((comps, depth + 4, rows + 16, cols), f32),
            vm(fine_prev.shape, f32),
            vm(fine_media.shape, f32),
            vm((comps, depth + 4, crows + 16, ccols), f32),
            vm(coarse_prev.shape, f32),
            vm(coarse_media.shape, f32),
            vm(entry, jnp.int32),
            vm(entry, jnp.int32),
            vm(entry, jnp.int32),
            vm(entry, f32),
            vm((2, comps, depth, 2, cols), f32),
            vm((2, comps, depth, 2, cols), f32),
            vm((2, rows, 128), f32),
            vm((2, rows, 128), f32),
            vm((2, comps, depth, 2, ccols), f32),
            vm((2, comps, depth, 2, ccols), f32),
            vm((2, crows, 128), f32),
            vm((2, crows, 128), f32),
            vm(entry, f32),
            vm(entry, f32),
            vm(entry, f32),
            vm(entry, f32),
            vm((2 * comps * n_gz * crows, ccols), f32),
            vm((comps, n_gz * crows, ccols), f32),
            vm((comps, crows, ccols), f32),
            pltpu.SemaphoreType.DMA((12,)),
            pltpu.SemaphoreType.DMA((9,)),
            pltpu.SemaphoreType.DMA((9,)),
        ],
        compiler_params=pltpu.CompilerParams(
            collective_id=0, has_side_effects=True, vmem_limit_bytes=32 * 1024 * 1024
        ),
    )(
        used_count,
        *(pltpu.with_memory_space_constraint(a, pltpu.HBM) for a in (fine_disp,
        fine_prev,
        fine_media,
        coarse_disp,
        coarse_prev,
        coarse_media,
        *lists)),
    )
    return pl.pallas_call(
        store,
        out_shape=out_shape,
        in_specs=[pl.BlockSpec(memory_space=pltpu.VMEM)] * 3,
        out_specs=(in_hbm,) * 3,
        scratch_shapes=[pltpu.SemaphoreType.DMA((3,))],
    )(*(pltpu.with_memory_space_constraint(a, pltpu.VMEM) for a in results))


def solution(mesh):
    sizes = (mesh.shape["gx"], mesh.shape["gy"], mesh.shape["gz"])
    fine = P(None, None, ("gy", "gz"), "gx")
    coarse = P(None, None, "gy", ("gx", "gz"))
    entry = P("gx", ("gy", "gz"), None)
    in_specs = (fine,) * 3 + (coarse,) * 3 + (entry,) * 4 + (P("gx", ("gy", "gz")),)
    out_specs = (fine, coarse, P(None, "gy", ("gx", "gz")))
    return jax.shard_map(
        functools.partial(shards, sizes),
        mesh=mesh,
        in_specs=in_specs,
        out_specs=out_specs,
        check_vma=False,
    )
```

profile of v0, /device:TPU:9, one launch (start us, length us, event | category | flops | bytes accessed | tf_op | source)
XLA Modules:
  0.0 15.3 jit_solution(17474470445447684825)
XLA Ops:
  1.3 13.1 %shard_map.130 = (f32[3,8,16,512]{3,2,1,0:T(8,128)S(1)}, f32[3,8,16,128]{3,2,1,0:T(8,128)S(1)}, f32[3,16,128]{2,1,0:T(8,128)S(1)}) custom-call(s32[1,1]{1,0:T(1,128)S(6)} %copy.14.count_hbm, f32[3,8,16,512]{3,2,1,0:T(8,128)} %fine_hbm.1, f32[3,8,16,512]{3,2,1,0:T(8,128)} %fprev_hbm.1, f32[4,8,16,512]{3,2,1,0:T(8,128)} %fmedia_hbm.1, ...), custom_call_target="tpu_custom_call" | custom-call | tf_op jit(solution)/shard_map/pallas_call | solution.py:395
  14.4 1.0 %shard_map.131 = (f32[3,8,16,512]{3,2,1,0:T(8,128)}, f32[3,8,16,128]{3,2,1,0:T(8,128)}, f32[3,16,128]{2,1,0:T(8,128)}) custom-call(f32[3,8,16,512]{3,2,1,0:T(8,128)S(1)} %get-tuple-element.6.fnext, f32[3,8,16,128]{3,2,1,0:T(8,128)S(1)} %get-tuple-element.7.cnext, f32[3,16,128]{2,1,0:T(8,128)S(1)} %get-tuple-element.8.ghost), custom_call_target="tpu_custom_call" | custom-call | tf_op jit(solution)/shard_map/pallas_call | solution.py:444
where the time goes:
time: 15.5 us; the launch traced here: 15.3 us
  Pallas kernels  14.1 us (91%)
  between operations  1.29 us (8%)
    pallas_call x1, Pallas kernels, shards(): pl.pallas_call(functools.partial(kernel, sizes), out_shape=tuple((vm(o.sh...  13.1 us
    pallas_call x1, Pallas kernels, shards(): pl.pallas_call(store, out_shape=out_shape, in_specs=[pl.BlockSpec(memory_...  0.97 us

commit v1 on v0

--- a/solution.py
+++ b/solution.py
@@ -34,14 +34,12 @@
     out_ref[...] = total
 
 
-def stencil_xy(ref, from_low, from_high, c, z, k):
-    rows = from_low.shape[0]
+def stencil_xy(ref, rows, c, z):
     cols = ref.shape[3]
     wide = cols + 256
     mid = ref[c, 2 + z, 8 : 8 + rows, :]
-    left = pltpu.roll(from_low[...], 126 - 2 * k, 1)
-    right = pltpu.roll(from_high[...], (128 - 2 * k) % 128, 1)
-    ext = jnp.concatenate([left, mid, right], axis=1)
+    edge = jnp.zeros((rows, 128), jnp.float32)
+    ext = jnp.concatenate([edge, mid, edge], axis=1)
     moved = [pltpu.roll(ext, s % wide, 1)[:, 128 : 128 + cols] for s in (2, 1, -1, -2)]
     along_x = second((moved[0], moved[1], mid, moved[2], moved[3]))
     shifted = [ref[c, 2 + z, 6 + s : 6 + s + rows, :] for s in (0, 1, 3, 4)]
@@ -56,6 +54,40 @@
         )
     )
     return mid, along_x, along_y, along_z
+
+
+def add_halos(out, media, y_in, x_in, step):
+    comps, depth, rows, cols = out.shape
+    row = lax.broadcasted_iota(jnp.int32, (8, cols), 0)
+    lane = lax.broadcasted_iota(jnp.int32, (rows, 128), 1)
+    twelfth = 1.0 / 12.0
+    for z in range(depth):
+        shear, first, density = (media[i, z] for i in range(3))
+        scale = step / density
+        plain = scale * shear
+        full = plain + scale * (first + shear)
+        for c in range(comps):
+            k = c * depth + z
+            factor = full if c == 1 else plain
+            outer, inner = y_in[0, c, z, 0:1, :], y_in[0, c, z, 1:2, :]
+            low = jnp.where(row == 1, -twelfth * inner, 0.0)
+            low = jnp.where(row == 0, (16.0 * inner - outer) * twelfth, low)
+            inner, outer = y_in[1, c, z, 0:1, :], y_in[1, c, z, 1:2, :]
+            high = jnp.where(row == 6, -twelfth * inner, 0.0)
+            high = jnp.where(row == 7, (16.0 * inner - outer) * twelfth, high)
+            out[c, z, 0:8, :] += factor[0:8] * low
+            out[c, z, rows - 8 : rows, :] += factor[rows - 8 : rows] * high
+            factor = full if c == 0 else plain
+            near = pltpu.roll(x_in[0], (127 - 2 * k) % 128, 1)
+            both = pltpu.roll(x_in[0], (128 - 2 * k) % 128, 1)
+            low = jnp.where(lane == 1, -twelfth * both, 0.0)
+            low = jnp.where(lane == 0, (16.0 * near - both) * twelfth, low)
+            near = pltpu.roll(x_in[1], (127 - 2 * k) % 128, 1)
+            both = pltpu.roll(x_in[1], (126 - 2 * k) % 128, 1)
+            high = jnp.where(lane == 126, -twelfth * both, 0.0)
+            high = jnp.where(lane == 127, (16.0 * near - both) * twelfth, high)
+            out[c, z, :, 0:128] += factor[:, 0:128] * low
+            out[c, z, :, cols - 128 : cols] += factor[:, cols - 128 : cols] * high
 
 
 def kernel(
@@ -297,10 +329,9 @@
         def _():
             halo(n).wait_recv()
 
-    for n in range(4):
-        arrive(n)
-    fp[:, 2 : 2 + depth, 6:8, :] = fy_in[0]
-    fp[:, 2 : 2 + depth, 8 + rows : 10 + rows, :] = fy_in[1]
+    edge_rows = jnp.zeros((comps, depth, 2, cols), jnp.float32)
+    fp[:, 2 : 2 + depth, 6:8, :] = edge_rows
+    fp[:, 2 : 2 + depth, 8 + rows : 10 + rows, :] = edge_rows
     load[8].wait()
     load[9].wait()
     for z in range(depth):
@@ -308,17 +339,15 @@
         scale = step_scale / density
         both = first + shear
         for c in range(comps):
-            k = c * depth + z
-            mid, along_x, along_y, along_z = stencil_xy(fp, fx_in.at[0], fx_in.at[1], c, z, k)
+            mid, along_x, along_y, along_z = stencil_xy(fp, rows, c, z)
             along_z = metric * along_z
             along = (along_x, along_y, along_z)[c]
             accel = shear * (along_x + along_y + along_z) + both * along
             fnext[c, z] = 2.0 * mid - fprev[c, z] + scale * accel
 
-    for n in range(4, 8):
-        arrive(n)
-    cp[:, 2 : 2 + depth, 6:8, :] = cy_in[0]
-    cp[:, 2 : 2 + depth, 8 + crows : 10 + crows, :] = cy_in[1]
+    edge_rows = jnp.zeros((comps, depth, 2, ccols), jnp.float32)
+    cp[:, 2 : 2 + depth, 6:8, :] = edge_rows
+    cp[:, 2 : 2 + depth, 8 + crows : 10 + crows, :] = edge_rows
     load[10].wait()
     load[11].wait()
     for z in range(depth):
@@ -326,11 +355,15 @@
         scale = (step_scale / 4.0) / density
         both = first + shear
         for c in range(comps):
-            k = c * depth + z
-            mid, along_x, along_y, along_z = stencil_xy(cp, cx_in.at[0], cx_in.at[1], c, z, k)
+            mid, along_x, along_y, along_z = stencil_xy(cp, crows, c, z)
             along = (along_x, along_y, along_z)[c]
             accel = shear * (along_x + along_y + along_z) + both * along
             cnext[c, z] = 2.0 * mid - cprev[c, z] + scale * accel
+
+    for n in range(8):
+        arrive(n)
+    add_halos(fnext, fmedia, fy_in, fx_in, step_scale)
+    add_halos(cnext, cmedia, cy_in, cx_in, step_scale / 4.0)
 
     swap.wait_recv()
     own = pl.ds(pl.multiple_of(gz * crows, 8), crows)

time: 15.5 us -> 12.6 us (0.81)
  the two profiles are of different devices: /device:TPU:9 before, /device:TPU:0 now
where the time goes in v1:
time: 12.6 us; the launch traced here: 12.5 us
  Pallas kernels  11.2 us (89%)
  between operations  1.29 us (10%)
    pallas_call x1, Pallas kernels, shards(): pl.pallas_call(functools.partial(kernel, sizes), out_shape=tuple((vm(o.sh...  10.2 us
    pallas_call x1, Pallas kernels, shards(): pl.pallas_call(store, out_shape=out_shape, in_specs=[pl.BlockSpec(memory_...  0.97 us

profile of v1, /device:TPU:0, one launch (start us, length us, event | category | flops | bytes accessed | tf_op | source)
XLA Modules:
  0.0 12.5 jit_solution(11512910562428084890)
XLA Ops:
  1.3 10.2 %shard_map.130 = (f32[3,8,16,512]{3,2,1,0:T(8,128)S(1)}, f32[3,8,16,128]{3,2,1,0:T(8,128)S(1)}, f32[3,16,128]{2,1,0:T(8,128)S(1)}) custom-call(s32[1,1]{1,0:T(1,128)S(6)} %copy.14.count_hbm, f32[3,8,16,512]{3,2,1,0:T(8,128)} %fine_hbm.1, f32[3,8,16,512]{3,2,1,0:T(8,128)} %fprev_hbm.1, f32[4,8,16,512]{3,2,1,0:T(8,128)} %fmedia_hbm.1, ...), custom_call_target="tpu_custom_call" | custom-call | tf_op jit(solution)/shard_map/pallas_call | solution.py:428
  11.5 1.0 %shard_map.131 = (f32[3,8,16,512]{3,2,1,0:T(8,128)}, f32[3,8,16,128]{3,2,1,0:T(8,128)}, f32[3,16,128]{2,1,0:T(8,128)}) custom-call(f32[3,8,16,512]{3,2,1,0:T(8,128)S(1)} %get-tuple-element.6.fnext, f32[3,8,16,128]{3,2,1,0:T(8,128)S(1)} %get-tuple-element.7.cnext, f32[3,16,128]{2,1,0:T(8,128)S(1)} %get-tuple-element.8.ghost), custom_call_target="tpu_custom_call" | custom-call | tf_op jit(solution)/shard_map/pallas_call | solution.py:477
